TPU v7x, 512 devices: a whole 4x8x8 slice. The times are simulated.
512 devices in a mesh: row: 16 (over y, core), col: 32 (over z, x).
Axes of the slice: x: 4, y: 8, z: 8, core: 2. Of those that a mesh axis runs over, the one named last changes fastest.
Arguments:
- old_vectors: float32 [8192, 4096], P('row', 'col'), may hold values from -6 to 6, as said below
- pole_values: float32 [8192], replicated, may hold values from 0 to 8192, as said below
- live_mask: int32 [8192], replicated, may hold values from 0 to 1, as said below
- position: int32 [8192], replicated, may hold values from 0 to 8191, as said below
- rank_weight: float32 [1], replicated, may hold values from 0.5 to 2
Outputs:
- new_vectors: float32 [8192, 8192], P('row', 'col')
Inputs may be any that keep to these rules, and one draw needn't show every extreme that they name: `pole_values`: strictly increasing; consecutive values differ by 0.2 or more. `old_vectors`: the entries of rows 4095 and 4096 have magnitude 0.5 to 1.5. Each merged position appears exactly once. In every aligned group of 16 consecutive columns s of the halves' eigenvectors (s = h * 4096 + m), exactly 12 have live_mask[position[s]] = 1.
All inputs are finite; a program needn't handle non-finite values.
Results may differ from a plain program's by a relative error of at most 0.0003.
Values sent between devices are 32-bit elements; how exact they have to be, the bound alone decides.
A program may use at most 64 MiB of HBM per device.

v0:
```python
import jax
import jax.numpy as jnp
from jax import lax
from jax.sharding import PartitionSpec as P

BISECT = 40


def bracket_lengths(pole_values, live_mask, squares, rank_value):
    order_size = pole_values.shape[0]
    positions = jnp.arange(order_size, dtype=jnp.int32)
    marked = jnp.where(live_mask > 0, positions, order_size)
    shifted = jnp.concatenate([marked[1:], jnp.full((1,), order_size, jnp.int32)])
    following = lax.cummin(shifted, axis=0, reverse=True)
    weight_sum = rank_value * jnp.sum(squares)
    next_gap = pole_values[jnp.minimum(following, order_size - 1)] - pole_values
    return jnp.where(following < order_size, next_gap, weight_sum)


def bisect_roots(pole_here, bracket_len, pole_values, squares, live_mask, rank_value):
    pole_diff = pole_values[None, :] - pole_here[:, None]
    alive_cols = (live_mask > 0)[None, :]

    def halving(interval, unused):
        low_end, high_end = interval
        middle = 0.5 * (low_end + high_end)
        offset_gap = pole_diff - middle[:, None]
        summands = jnp.where(
            alive_cols, squares[None, :] / jnp.where(alive_cols, offset_gap, 1.0), 0.0
        )
        secular = 1.0 + rank_value * jnp.sum(summands, axis=1)
        is_below = secular < 0.0
        return ((jnp.where(is_below, middle, low_end), jnp.where(is_below, high_end, middle)), None)

    interval, unused = lax.scan(
        halving, (jnp.zeros_like(bracket_len), bracket_len), None, length=BISECT
    )
    return 0.5 * (interval[0] + interval[1])


def log_terms(pole_here, offsets, live_here, own_index, pole_values, live_mask):
    order_size = pole_values.shape[0]
    pole_diff = pole_values[None, :] - pole_here[:, None]
    on_pole = own_index[:, None] == jnp.arange(order_size, dtype=jnp.int32)[None, :]
    quotient = jnp.where(
        on_pole, offsets[:, None], 1.0 - offsets[:, None] / jnp.where(on_pole, 1.0, pole_diff)
    )
    in_play = (live_here[:, None] > 0) & (live_mask[None, :] > 0)
    logs = jnp.where(in_play, jnp.log(jnp.abs(jnp.where(in_play, quotient, 1.0))), 0.0)
    return jnp.sum(logs, axis=0)


def column_norms(pole_here, offsets, live_here, pole_values, live_mask, hat_weights):
    alive_cols = (live_mask > 0)[None, :]
    offset_gap = pole_values[None, :] - pole_here[:, None] - offsets[:, None]
    summands = jnp.where(
        alive_cols, hat_weights[None, :] ** 2 / jnp.where(alive_cols, offset_gap, 1.0) ** 2, 0.0
    )
    return jnp.where(live_here > 0, jnp.sqrt(jnp.sum(summands, axis=1)), 1.0)


def cauchy_tile(
    sorted_rows,
    pole_cols,
    offset_cols,
    norm_cols,
    live_cols,
    col_index,
    pole_values,
    live_mask,
    hat_weights,
):
    row_poles = pole_values[sorted_rows]
    row_hats = hat_weights[sorted_rows]
    row_live = live_mask[sorted_rows] > 0
    col_live = (live_cols > 0)[None, :]
    both_live = row_live[:, None] & col_live
    offset_gap = row_poles[:, None] - pole_cols[None, :] - offset_cols[None, :]
    entries = row_hats[:, None] / jnp.where(both_live, offset_gap, 1.0) / norm_cols[None, :]
    identity = (sorted_rows[:, None] == col_index[None, :]).astype(jnp.float32)
    return jnp.where(col_live, jnp.where(both_live, entries, 0.0), identity)


def hat_from(log_sum, coupling, live_mask, rank_value):
    return jnp.where(
        live_mask > 0, jnp.sign(coupling) * jnp.exp(0.5 * (log_sum - jnp.log(rank_value))), 0.0
    )


def shards(old_vectors, pole_values, live_mask, position, rank_weight):
    rank_value = rank_weight[0]
    order_size = pole_values.shape[0]
    half_order = order_size // 2
    rows_here = old_vectors.shape[0]
    row_count = lax.axis_size("row")
    col_count = lax.axis_size("col")
    row_rank = lax.axis_index("row")
    col_rank = lax.axis_index("col")
    upper_owner = (half_order - 1) // rows_here
    lower_owner = half_order // rows_here
    edge_rows = jnp.stack(
        [
            jnp.where(row_rank == upper_owner, old_vectors[(half_order - 1) % rows_here], 0.0),
            jnp.where(row_rank == lower_owner, old_vectors[half_order % rows_here], 0.0),
        ]
    )
    edge_rows = lax.psum(edge_rows, "row")
    edge_rows = lax.all_gather(edge_rows, "col", axis=1, tiled=True)
    boundary = jnp.concatenate([edge_rows[0], edge_rows[1]])
    spread = jnp.zeros((order_size,), jnp.float32).at[position].set(boundary)
    coupling = jnp.where(live_mask > 0, spread, 0.0)
    squares = coupling * coupling
    bracket_len = bracket_lengths(pole_values, live_mask, squares, rank_value)
    block_cols = order_size // col_count
    per_device = block_cols // row_count
    block_first = col_rank * block_cols
    own_first = block_first + row_rank * per_device
    block_index = block_first + jnp.arange(block_cols, dtype=jnp.int32)
    own_poles = lax.dynamic_slice_in_dim(pole_values, own_first, per_device)
    own_live = lax.dynamic_slice_in_dim(live_mask, own_first, per_device)
    own_bracket = lax.dynamic_slice_in_dim(bracket_len, own_first, per_device)
    block_poles = lax.dynamic_slice_in_dim(pole_values, block_first, block_cols)
    block_live = lax.dynamic_slice_in_dim(live_mask, block_first, block_cols)
    bisected = bisect_roots(own_poles, own_bracket, pole_values, squares, live_mask, rank_value)
    own_offsets = jnp.where(own_live > 0, bisected, 0.5 * own_bracket)
    block_offsets = lax.all_gather(own_offsets, "row", axis=0, tiled=True)
    grouped = (
        block_poles.reshape(row_count, per_device),
        block_offsets.reshape(row_count, per_device),
        block_live.reshape(row_count, per_device),
        block_index.reshape(row_count, per_device),
    )

    def log_group(members):
        return log_terms(members[0], members[1], members[2], members[3], pole_values, live_mask)

    partial_logs = jnp.sum(lax.map(log_group, grouped), axis=0)
    log_sum = lax.psum(partial_logs, "col")
    hat_weights = hat_from(log_sum, coupling, live_mask, rank_value)

    def norm_group(members):
        return column_norms(members[0], members[1], members[2], pole_values, live_mask, hat_weights)

    block_norms = lax.map(norm_group, (grouped[0], grouped[1], grouped[2])).reshape(block_cols)
    half_id = row_rank * rows_here // half_order
    half_base = half_id * half_order
    panel_piece = lax.all_gather(old_vectors, "col", axis=1, tiled=True)
    sorted_rows = lax.dynamic_slice_in_dim(position, half_base, panel_piece.shape[1])
    cauchy = cauchy_tile(
        sorted_rows,
        block_poles,
        block_offsets,
        block_norms,
        block_live,
        block_index,
        pole_values,
        live_mask,
        hat_weights,
    )
    return jnp.dot(
        panel_piece, cauchy, precision=lax.Precision.HIGHEST, preferred_element_type=jnp.float32
    )


def solution(mesh):
    in_specs = (P("row", "col"), P(), P(), P(), P())
    out_specs = P("row", "col")
    return jax.shard_map(shards, mesh=mesh, in_specs=in_specs, out_specs=out_specs, check_vma=False)
```

profile of v0, /device:TPU:6, one launch (start us, length us, event | category | flops | bytes accessed | tf_op | source)
XLA Modules:
  0.0 486.6 jit_solution(11255109670068731941)
XLA Ops:
  6.5 0.7 all-gather.2.cloned.1.call-update
  7.3 0.7 broadcast_select_fusion.2
  8.0 26.4 %psum.14 = f32[2,128]{1,0:T(2,128)S(1)} all-reduce(f32[2,128]{1,0:T(2,128)S(1)} %pad_maximum_fusion.1), channel_id=1, replica_groups=mesh['row'=16,'col'=32] {'row'}, use_global_device_ids=true, to_apply=%region_0.1 | all-reduce | flops 256 | bytes 2048 | tf_op jit(solution)/shard_map/psum | solution.py:107
  34.4 48.6 %all_gather.9 = f32[2,4096]{1,0:T(2,128)S(1)} all-gather(f32[2,128]{1,0:T(2,128)S(1)} %psum.14), channel_id=1, replica_groups=mesh['row'=16,'col'=32] {'col'}, dimensions={1}, use_global_device_ids=true | all-gather | bytes 33792 | tf_op jit(solution)/shard_map/all_gather | solution.py:108
  83.1 0.8 compare_select_fusion.4
  83.9 30.5 %scatter_custom_fusion = f32[8192]{0:T(1024)S(1)} fusion(s32[8192]{0:T(1024)S(1)} %compare_select_fusion.4, f32[8192]{0:T(1024)S(1)} %pad_maximum_fusion, f32[]{:T(128)} %constant.114.clone.1), kind=kCustom, calls=%fused_computation.74 | custom fusion | bytes 32772 | tf_op jit(solution)/shard_map/scatter | solution.py:110
  114.3 1.4 fusion.44
  115.9 2.3 reduce-window.9
  119.2 0.8 broadcast_compare_fusion.4
  120.0 0.8 dynamic_slice.52
  120.8 45.5 %gather_fusion.1 = f32[8192]{0:T(1024)S(1)} fusion(f32[8192]{0:T(1024)S(1)} %copy-done, s32[8192]{0:T(1024)S(1)} %broadcast_clamp_fusion), kind=kCustom, calls=%fused_computation.1 | custom fusion | bytes 98304 | tf_op jit(solution)/shard_map/gather | solution.py:16
  167.6 46.3 %while.37 = (s32[]{:T(128)}, f32[16]{0:T(128)S(1)}, f32[16]{0:T(128)S(1)}, f32[]{:T(128)}, pred[1,8192]{1,0:T(4,128)(4,1)S(1)}, /*index=5*/f32[8192]{0:T(1024)S(...) while((s32[]{:T(128)}, f32[16]{0:T(128)S(1)}, ...), condition=%wide.region_7.8_spmd.clone, body=%wide.region_5.7_spmd.clone.sunk | while | flops 786563 | bytes 91005 | solution.py:35
  168.1 0.7 compare_select_fusion.10
  169.2 0.7 compare_select_fusion.10
  170.4 0.7 compare_select_fusion.10
  171.6 0.7 compare_select_fusion.10
  172.7 0.7 compare_select_fusion.10
  173.9 0.7 compare_select_fusion.10
  175.0 0.7 compare_select_fusion.10
  176.2 0.7 compare_select_fusion.10
  185.5 0.7 compare_select_fusion.10
  207.5 0.7 compare_select_fusion.10
  214.0 1.3 dynamic-slice
  216.1 23.5 %all-reduce = f32[256]{0:T(256)S(1)} all-reduce(f32[256]{0:T(256)S(1)} %fusion.40), channel_id=1, replica_groups=mesh['row'=16,'col'=32] {'row'}, use_global_device_ids=true, to_apply=%add | all-reduce | flops 256 | bytes 2048
  239.8 10.5 %while.35 = (s32[]{:T(128)}, f32[16,8192]{1,0:T(8,128)S(1)}, s32[16,16]{1,0:T(8,128)S(1)}, s32[8192]{0:T(1024)S(1)}, s32[16,16]{1,0:T(8,128)S(1)}, /*index=5*/f3...) while((s32[]{:T(128)}, f32[16,8192]{1,0:T(8,128)S(1)}, ...), condition=%wide.region_10.11_spmd, body=%wide.region_8.10_spmd.sunk | while | flops 1441810 | bytes 181013 | solution.py:137
  250.4 23.0 %gather_fusion = s32[4096]{0:T(1024)S(1)} fusion(s32[8192]{0:T(1024)S(1)} %get-tuple-element.538, s32[4096]{0:T(1024)S(1)} %get-tuple-element.264), kind=kCustom, calls=%fused_computation | custom fusion | bytes 49152 | tf_op jit(solution)/shard_map/gather | solution.py:75
  273.4 23.0 %gather_fusion.3 = f32[4096]{0:T(1024)S(1)} fusion(f32[8192]{0:T(1024)S(1)} %get-tuple-element.537, s32[4096]{0:T(1024)S(1)} %get-tuple-element.264), kind=kCustom, calls=%fused_computation.3 | custom fusion | bytes 49152 | tf_op jit(solution)/shard_map/gather | solution.py:73
  296.6 131.6 %psum.15 = f32[8192]{0:T(1024)S(1)} all-reduce(f32[8192]{0:T(1024)S(1)} %reduce_sum.48), channel_id=1, replica_groups=mesh['row'=16,'col'=32] {'col'}, use_global_device_ids=true, to_apply=%region_12.13 | all-reduce | flops 8192 | bytes 65536 | tf_op jit(solution)/shard_map/psum | solution.py:138
  428.3 23.0 %gather_fusion.2 = f32[4096]{0:T(1024)S(1)} fusion(f32[8192]{0:T(1024)S(1)} %get-tuple-element.267, s32[4096]{0:T(1024)S(1)} %get-tuple-element.264), kind=kCustom, calls=%fused_computation.2 | custom fusion | bytes 49152 | tf_op jit(solution)/shard_map/gather | solution.py:74
  451.3 8.1 %while.36 = (s32[]{:T(128)}, f32[16,16]{1,0:T(8,128)S(1)}, s32[16,16]{1,0:T(8,128)S(1)}, s32[8192]{0:T(1024)S(1)}, f32[1,8192]{1,0:T(1,128)S(1)}, /*index=5*/f32...) while((s32[]{:T(128)}, f32[16,16]{1,0:T(8,128)S(1)}, ...), condition=%wide.region_15.16_spmd, body=%wide.region_13.15_spmd.sunk | while | flops 925714 | bytes 115569 | solution.py:144
  459.5 19.3 %fusion.34 = f32[512,256]{0,1:T(8,128)S(1)} fusion(f32[512,4096]{1,0:T(8,128)} %all-gather.2.cloned.1.call-done, s32[256]{0:T(256)S(1)} %iota_add_fusion, f32[256]{0:T(256)S(1)} %div.58, f32[256]{0:T(256)S(1)} %all-reduce, f32[256]{0:T(256)S(1)} %dynamic_slice.52, f32[4096]{0:T(1024)S(1)} %gather_fusion.3, f32[4096]{0:T(1024)S(1)} %gather_fusion.2, ...), kind=kOutput, calls=%fused_computation.60 | convolution fusion | flops 6452936704 | bytes 8970496 | tf_op jit(solution)/shard_map/dot_general | solution.py:160
  478.8 1.0 copy.8
  (363 shorter events, 57.5 us)
Async XLA Ops:
  6.5 114.2 %copy-start = (f32[8192]{0:T(1024)S(1)}, f32[8192]{0:T(1024)}, u32[]{:S(2)}) copy-start(f32[8192]{0:T(1024)} %param.12) | copy-start | bytes 98308
  6.5 452.9 %all-gather.2.cloned.1.call-start = ((), (), s32[]{:S(2)}) async-start(), calls=%async_computation | async-start | bytes 8650752 | tf_op jit(solution)/shard_map/all_gather | solution.py:147
  120.8 95.1 %copy-start.1 = (s32[8192]{0:T(1024)S(1)}, s32[8192]{0:T(1024)}, u32[]{:S(2)}) copy-start(s32[8192]{0:T(1024)} %param.13) | copy-start | bytes 98308
  120.8 129.6 %copy-start.2 = (s32[8192]{0:T(1024)S(1)}, s32[8192]{0:T(1024)}, u32[]{:S(2)}) copy-start(s32[8192]{0:T(1024)} %param.14) | copy-start | bytes 98308
Sparse Core Ops, SparseCore 0:
  10.4 113.5 all-gather.1
where the time goes:
time: 494 us; the launch traced here: 487 us
  blocking collectives  230 us (47%)
  local copies, waits for them, and re-layouts  152 us (31%)
  other arithmetic  65.8 us (13%)
  matrix products  19.3 us (4%)
  between operations  15.6 us (3%)
    psum x1, blocking collectives, shards(): log_sum = lax.psum(partial_logs, 'col')  132 us
    all_gather x1, blocking collectives, shards(): edge_rows = lax.all_gather(edge_rows, 'col', axis=1, tiled=True)  48.6 us
    gather x1, local copies, waits for them, and re-layouts, bracket_lengths(): next_gap = pole_values[jnp.minimum(following, order_size - 1)] - pole_values  45.5 us
    scatter x1, local copies, waits for them, and re-layouts, shards(): spread = jnp.zeros((order_size,), jnp.float32).at[position].set(boundary)  30.5 us
    psum x1, blocking collectives, shards(): edge_rows = lax.psum(edge_rows, 'row')  26.4 us
    select_n x40, other arithmetic, halving(): jnp.where(is_below, high_end, middle)  26.3 us
    unnamed x1, blocking collectives  23.5 us
    gather x1, local copies, waits for them, and re-layouts, cauchy_tile(): row_live = live_mask[sorted_rows] > 0  23 us
  transfers between devices with their start and end apart: 1, of which 0 were waited for; matrix products, arithmetic and copies ran while one was open for 45% of the time, Pallas kernels for 0%

commit v1 on v0

v1 whole, which is shorter than its diff:
```python
import functools

import jax
import jax.numpy as jnp
from jax import lax
from jax.experimental import pallas as pl
from jax.experimental.pallas import tpu as pltpu
from jax.sharding import PartitionSpec as P

F32 = jnp.float32
BF16 = jnp.bfloat16
MESH = pl.DeviceIdType.MESH
FAR = 1e30
FAR_TEST = 1e29
ROOT_STEPS = 7
NR, NC, NZ, NX = 16, 32, 8, 4
ROWS, COLS = 512, 128
OUT = 256
OWN = OUT // NR
HALF_ROWS = ROWS // 2


def reciprocal(x):
    r = pl.reciprocal(x, approx=True)
    r = r * (2.0 - x * r)
    return r * (2.0 - x * r)


def kernel(
    x_ref, pole_ref, live_ref, posn_ref, rank_ref, out_ref,
    panel, buf1, buf2, buf3, buf4, buf5,
    djb, ljb, kp, kd, kl, npole, nsq, nsg, dd, bracket_ref,
    ah, al, ch, cl, tx, rx, norm_ref,
    s1, s2s, s2r, s3s, s3r, s4s, s4r, s5s, s5r,
    own_sem, os, orr, xs, xr, zs, zr, rs, rr, s1s,
):
    r = lax.axis_index("row")
    c = lax.axis_index("col")
    z = c // NX
    x = lax.rem(c, NX)
    h = r // (NR // 2)
    rho = rank_ref[0]

    def col_dev(dz, dx):
        return (r, lax.rem(z + dz + NZ, NZ) * NX + lax.rem(x + dx + NX, NX))

    barrier = pltpu.get_barrier_semaphore()
    for k in range(1, NC):
        pl.semaphore_signal(barrier, inc=1, device_id=(r, lax.rem(c + k, NC)), device_id_type=MESH)
    for k in range(1, NR):
        pl.semaphore_signal(barrier, inc=1, device_id=(lax.rem(r + k, NR), c), device_id_type=MESH)

    own_copy = pltpu.make_async_copy(x_ref, panel.at[0, z], own_sem)
    own_copy.start()

    for q in range(2):
        prow = pole_ref[pl.ds(2 * c + q, 1), :]
        djb[q * 128:(q + 1) * 128, :] = jnp.transpose(jnp.broadcast_to(prow, (128, 128)))
        lrow = live_ref[pl.ds(2 * c + q, 1), :].astype(F32)
        ljb[q * 128:(q + 1) * 128, :] = jnp.transpose(jnp.broadcast_to(lrow, (128, 128)))

    pos = jnp.concatenate(
        [posn_ref[pl.ds(c, 1), :], posn_ref[pl.ds(NC + c, 1), :]], axis=1
    )
    table = jnp.transpose(pole_ref[...])
    t0 = table.astype(BF16)
    rest = table - t0.astype(F32)
    t1 = rest.astype(BF16)
    t2 = (rest - t1.astype(F32)).astype(BF16)
    tl = jnp.transpose(live_ref[...].astype(F32)).astype(BF16)
    tables = jnp.concatenate([t0, t1, t2, tl], axis=0)
    high = lax.broadcasted_iota(jnp.int32, (64, 256), 0) == (pos >> 7)
    picked = jnp.dot(tables, jnp.where(high, 1.0, 0.0).astype(BF16), preferred_element_type=F32)
    low = lax.broadcasted_iota(jnp.int32, (128, 256), 0) == (pos & 127)
    pole_s = jnp.sum(
        jnp.where(low, (picked[0:128] + picked[128:256]) + picked[256:384], 0.0), axis=0, keepdims=True
    )
    live_s = jnp.sum(jnp.where(low, picked[384:512], 0.0), axis=0, keepdims=True)
    buf2[c, :, :] = jnp.zeros((8, 128), F32)
    buf2[c, 2:3, :] = pole_s[:, 0:128]
    buf2[c, 3:4, :] = pole_s[:, 128:256]
    buf2[c, 4:5, :] = live_s[:, 0:128]
    buf2[c, 5:6, :] = live_s[:, 128:256]

    pl.semaphore_wait(barrier, NR - 1 + NC - 1)

    def boundary_copy(q, k):
        src = x_ref.at[pl.ds(ROWS - 8, 8)] if q == 0 else x_ref.at[pl.ds(0, 8)]
        return pltpu.make_async_remote_copy(
            src_ref=src, dst_ref=buf1.at[q], send_sem=s1s.at[k - 1], recv_sem=s1.at[q],
            device_id=(lax.rem(r + k, NR), c), device_id_type=MESH,
        )

    for q, owner in ((0, NR // 2 - 1), (1, NR // 2)):
        @pl.when(r == owner)
        def _():
            for k in range(1, NR):
                boundary_copy(q, k).start()
            buf1[q, :, :] = x_ref[ROWS - 8:ROWS, :] if q == 0 else x_ref[0:8, :]

    up, down = col_dev(1, 0), col_dev(-1, 0)
    across = col_dev(0, 2)

    def part(k):
        return pl.ds(k * HALF_ROWS, HALF_ROWS)

    def own_line(d, s, k):
        block = lax.rem(z - s + NZ, NZ) if d == 0 else lax.rem(z + s, NZ)
        src = x_ref.at[part(k)] if s == 0 else panel.at[0, block, part(k)]
        return pltpu.make_async_remote_copy(
            src_ref=src, dst_ref=panel.at[0, block, part(k)], send_sem=os.at[d, s, k],
            recv_sem=orr.at[d, s, k], device_id=up if d == 0 else down, device_id_type=MESH,
        )

    def over_x(i, k):
        block = lax.rem(z + (0, -1, 1)[i] + NZ, NZ)
        src = x_ref.at[part(k)] if i == 0 else panel.at[0, block, part(k)]
        return pltpu.make_async_remote_copy(
            src_ref=src, dst_ref=panel.at[1, block, part(k)], send_sem=xs.at[i, k],
            recv_sem=xr.at[i, k], device_id=across, device_id_type=MESH,
        )

    def x_line(d, s, k):
        block = lax.rem(z - s + NZ, NZ) if d == 0 else lax.rem(z + s, NZ)
        return pltpu.make_async_remote_copy(
            src_ref=panel.at[1, block, part(k)], dst_ref=panel.at[1, block, part(k)],
            send_sem=zs.at[d, s - 1, k], recv_sem=zr.at[d, s - 1, k],
            device_id=up if d == 0 else down, device_id_type=MESH,
        )

    for k in range(2):
        for d in range(2):
            own_line(d, 0, k).start()
        over_x(0, k).start()

    @pl.when(r != NR // 2 - 1)
    def _():
        boundary_copy(0, 1).wait_recv()

    @pl.when(r != NR // 2)
    def _():
        boundary_copy(1, 1).wait_recv()

    buf2[c, 0:1, :] = buf1[0, 7:8, :]
    buf2[c, 1:2, :] = buf1[1, 0:1, :]

    def spread(buf, n, send, recv, along_row):
        me = r if along_row else c
        order = sorted(range(1, n), key=lambda k: -min(k, n - k))
        for k in order:
            peer = lax.rem(me + k, n)
            pltpu.make_async_remote_copy(
                src_ref=buf.at[me], dst_ref=buf.at[me], send_sem=send, recv_sem=recv,
                device_id=(peer, c) if along_row else (r, peer), device_id_type=MESH,
            ).start()

    def settle(buf, n, sem):
        some = buf.at[pl.ds(0, n - 1)]
        pltpu.make_async_copy(some, some, sem).wait()

    spread(buf2, NC, s2s, s2r, False)

    own_first = pl.multiple_of(r * OWN, OWN)
    dj = djb[pl.ds(own_first, OWN), :]
    nearest = jnp.full((OWN, 128), FAR, F32)
    for k in range(64):
        apole = jnp.where(live_ref[k:k + 1, :] > 0, pole_ref[k:k + 1, :], FAR)
        gap = apole - dj
        nearest = jnp.minimum(nearest, jnp.where(gap > 0.0, gap, FAR))
    bracket_ref[...] = jnp.broadcast_to(jnp.min(nearest, axis=1, keepdims=True), (OWN, 128))

    for k in range(2):
        for d in range(2):
            own_line(d, 0, k).wait_recv()
            own_line(d, 1, k).start()
        for i in (1, 2):
            over_x(i, k).start()

    settle(buf2, NC, s2r)

    bound = jnp.concatenate([buf2[:, 0, :], buf2[:, 1, :]], axis=0)
    praw = jnp.concatenate([buf2[:, 2, :], buf2[:, 3, :]], axis=0)
    alive = jnp.concatenate([buf2[:, 4, :], buf2[:, 5, :]], axis=0) > 0.5
    coupling = jnp.where(alive, bound, 0.0)
    nsq[...] = coupling * coupling
    nsg[...] = jnp.where(coupling > 0.0, 1.0, jnp.where(coupling < 0.0, -1.0, 0.0))
    npole[...] = jnp.where(alive, praw, FAR)

    weight_sum = rho * jnp.sum(nsq[...], axis=(0, 1), keepdims=True)
    near = bracket_ref[:, 0:1]
    bracket = jnp.where(near < FAR_TEST, near, weight_sum)
    for k in range(64):
        dd[:, k * 128:(k + 1) * 128] = npole[k:k + 1, :] - dj

    def root_step(_, carry):
        t, lo, hi = carry
        tb = jnp.broadcast_to(t, (OWN, 128))
        zero = jnp.zeros((OWN, 128), F32)
        psi, phi, dpsi, dphi = zero, zero, zero, zero
        for k in range(64):
            q = reciprocal(dd[:, k * 128:(k + 1) * 128] - tb)
            w = nsq[k:k + 1, :] * q
            dw = w * q
            below = w < 0.0
            psi = psi + jnp.where(below, w, 0.0)
            phi = phi + jnp.where(below, 0.0, w)
            dpsi = dpsi + jnp.where(below, dw, 0.0)
            dphi = dphi + jnp.where(below, 0.0, dw)
        psi = jnp.sum(psi, axis=1, keepdims=True)
        phi = jnp.sum(phi, axis=1, keepdims=True)
        dpsi = jnp.sum(dpsi, axis=1, keepdims=True)
        dphi = jnp.sum(dphi, axis=1, keepdims=True)
        secular = 1.0 + rho * (psi + phi)
        is_below = secular < 0.0
        lo = jnp.where(is_below, t, lo)
        hi = jnp.where(is_below, hi, t)
        e = bracket - t
        lower = rho * t * t * dpsi
        upper = rho * e * e * dphi
        level = 1.0 + rho * ((psi + t * dpsi) + (phi - e * dphi))
        linear = level * bracket + lower + upper
        constant = lower * bracket
        side = level * bracket - lower + upper
        spread_root = jnp.sqrt(side * side + 4.0 * lower * upper)
        positive = linear > 0.0
        top = jnp.where(positive, 2.0 * constant, linear - spread_root)
        under = jnp.where(positive, linear + spread_root, 2.0 * level)
        fresh = top / jnp.where(under == 0.0, 1.0, under)
        usable = (fresh > 0.0) & (fresh < bracket)
        fresh = jnp.where(usable, jnp.minimum(jnp.maximum(fresh, lo), hi), 0.5 * (lo + hi))
        return fresh, lo, hi

    start = 0.5 * bracket
    root, _, _ = lax.fori_loop(0, ROOT_STEPS, root_step, (start, jnp.zeros_like(start), bracket))
    own_live = ljb[pl.ds(own_first, OWN), :] > 0.5
    buf3[r, :, :] = jnp.where(own_live, jnp.broadcast_to(root, (OWN, 128)), jnp.broadcast_to(start, (OWN, 128)))
    spread(buf3, NR, s3s, s3r, True)

    for k in range(2):
        for d in range(2):
            own_line(d, 1, k).wait_recv()
            own_line(d, 2, k).start()

    settle(buf3, NR, s3r)

    for i in range(4):
        poles = npole[pl.ds(4 * r + i, 1), :]
        total = jnp.ones((8, 128), F32)
        for g in range(OUT // 8):
            d_j = djb[g * 8:(g + 1) * 8, :]
            off = buf3[g // 2, (g % 2) * 8:(g % 2) * 8 + 8, :]
            gap = poles - d_j
            ratio = (gap - off) * reciprocal(jnp.where(gap == 0.0, 1.0, gap))
            total = total * jnp.where(ljb[g * 8:(g + 1) * 8, :] > 0.5, jnp.abs(ratio), 1.0)
        total = total[0:4] * total[4:8]
        total = total[0:2] * total[2:4]
        buf4[c, i:i + 1, :] = total[0:1] * total[1:2]
    for q in range(2):
        tile = jnp.concatenate([buf3[q * 8 + g, :, :] for g in range(8)], axis=0)
        buf4[c, 4 + q:5 + q, :] = jnp.transpose(tile)[0:1, :]
    buf4[c, 6:8, :] = jnp.ones((2, 128), F32)
    spread(buf4, NC, s4s, s4r, False)

    own_line(0, 2, 0).wait_recv()
    own_line(0, 3, 0).start()
    own_line(1, 2, 1).wait_recv()
    own_line(1, 3, 1).start()
    for k in range(2):
        for d in range(2):
            over_x(1 + d, k).wait_recv()
            x_line(d, 1, k).start()
    own_line(0, 2, 1).wait_recv()
    own_line(1, 2, 0).wait_recv()

    for b in range(16):
        line = lax.rem(x + 2 * (b // 8), NX)
        source = (b % 8) * NX + line
        row = h * NC + source
        alive_row = buf2[source, pl.ds(4 + h, 1), :] > 0.5
        kp[b:b + 1, :] = npole[pl.ds(row, 1), :]
        place = posn_ref[pl.ds(row, 1), :].astype(F32)
        kd[b:b + 1, :] = jnp.where(alive_row, -1.0, place)
    kp[16:128, :] = jnp.zeros((112, 128), F32)
    kd[16:128, :] = jnp.zeros((112, 128), F32)
    kpt = jnp.transpose(kp[...])
    kdt = jnp.transpose(kd[...])
    kp[...] = kpt
    kd[...] = kdt

    def inverse_gaps(group, block, offs):
        for q in range(2):
            d_j = pole_ref[pl.ds(2 * block + q, 1), :]
            alive_j = live_ref[pl.ds(2 * block + q, 1), :] > 0
            off = offs[q]
            index = (lax.broadcasted_iota(jnp.int32, (1, 128), 1) + (block * OUT + q * 128)).astype(F32)
            for b in range(16):
                col = kp[:, b:b + 1]
                gap = (col - d_j) - off
                inverse = jnp.where(col < FAR_TEST, reciprocal(gap), 0.0)
                same = jnp.where(kd[:, b:b + 1] == index, 1.0, 0.0)
                value = jnp.where(alive_j, inverse, same)
                hi = value.astype(BF16)
                lo = (value - hi.astype(F32)).astype(BF16)
                ch[b * 128:(b + 1) * 128, group * OUT + q * 128:group * OUT + (q + 1) * 128] = hi
                cl[b * 128:(b + 1) * 128, group * OUT + q * 128:group * OUT + (q + 1) * 128] = lo

    settle(buf4, NC, s4r)
    product = buf4[0, :, :]
    for k in range(1, NC):
        product = product * buf4[k, :, :]
    first_rows = lax.broadcasted_iota(jnp.int32, (8, 128), 0) < 4
    product = jnp.where(first_rows, product, 1.0)
    buf5[r, :, :] = jnp.sqrt(product / rho)
    spread(buf5, NR, s5s, s5r, True)

    for k in range(2):
        for d in range(2):
            x_line(d, 1, k).wait_recv()
            x_line(d, 2, k).start()

    right = z * NX + lax.rem(x + 1, NX)
    left = z * NX + lax.rem(x + NX - 1, NX)
    for group, block in ((0, c), (1, right), (2, left)):
        inverse_gaps(group, block, [buf4[block, 4:5, :], buf4[block, 5:6, :]])

    settle(buf5, NR, s5r)

    def scaled(b):
        line = lax.rem(x + 2 * (b // 8), NX)
        row = h * NC + (b % 8) * NX + line
        hat = buf5[h * 8 + b % 8, pl.ds(line, 1), :] * nsg[pl.ds(row, 1), :]
        hat = jnp.where(npole[pl.ds(row, 1), :] < FAR_TEST, hat, 1.0)
        value = panel[b // 8, b % 8, :, :] * hat
        hi = value.astype(BF16)
        ah[:, b * 128:(b + 1) * 128] = hi
        al[:, b * 128:(b + 1) * 128] = (value - hi.astype(F32)).astype(BF16)

    own_copy.wait()
    own_line(0, 3, 0).wait_recv()
    own_line(1, 3, 1).wait_recv()
    for b in range(8):
        scaled(b)

    over_x(0, 0).wait_recv()
    over_x(0, 1).wait_recv()
    x_line(0, 2, 0).wait_recv()
    x_line(0, 3, 0).start()
    x_line(1, 2, 1).wait_recv()
    x_line(1, 3, 1).start()
    x_line(0, 2, 1).wait_recv()
    x_line(1, 2, 0).wait_recv()
    x_line(0, 3, 0).wait_recv()
    x_line(1, 3, 1).wait_recv()
    for b in range(8, 16):
        scaled(b)

    def product_of(first, count, group):
        rows = slice(first, first + count)
        cols = slice(group * OUT, (group + 1) * OUT)
        a_hi, a_lo = ah[rows, :], al[rows, :]
        c_hi, c_lo = ch[:, cols], cl[:, cols]
        return (
            jnp.dot(a_hi, c_lo, preferred_element_type=F32)
            + jnp.dot(a_lo, c_hi, preferred_element_type=F32)
        ) + jnp.dot(a_hi, c_hi, preferred_element_type=F32)

    def partial_copy(side):
        return pltpu.make_async_remote_copy(
            src_ref=tx.at[side], dst_ref=rx.at[side], send_sem=rs.at[side], recv_sem=rr.at[side],
            device_id=col_dev(0, 1 if side == 0 else -1), device_id_type=MESH,
        )

    for side in range(2):
        tx[side, :, :] = product_of(side * HALF_ROWS, HALF_ROWS, 1 + side)
        partial_copy(side).start()
    for side in range(2):
        out_ref[side * HALF_ROWS:(side + 1) * HALF_ROWS, :] = product_of(side * HALF_ROWS, HALF_ROWS, 0)

    def norm_group(g, _):
        first = pl.multiple_of(g * 8, 8)
        d_j = djb[pl.ds(first, 8), :]
        off = buf3[g // 2, pl.ds(pl.multiple_of(lax.rem(g, 2) * 8, 8), 8), :]
        total = jnp.zeros((8, 128), F32)
        for k in range(64):
            poles = npole[k:k + 1, :]
            hat = jnp.where(poles < FAR_TEST, buf5[k // 4, k % 4:k % 4 + 1, :], 0.0)
            w = hat * reciprocal((poles - d_j) - off)
            total = total + w * w
        norm_ref[pl.ds(first, 8), :] = total
        return 0

    lax.fori_loop(0, OUT // 8, norm_group, 0)
    scales = []
    for q in range(2):
        square = jnp.sum(jnp.transpose(norm_ref[q * 128:(q + 1) * 128, :]), axis=0, keepdims=True)
        alive_j = live_ref[pl.ds(2 * c + q, 1), :] > 0
        scales.append(jnp.where(alive_j, 1.0 / jnp.sqrt(jnp.where(alive_j, square, 1.0)), 1.0))
    scale = jnp.concatenate(scales, axis=1)

    for side in range(2):
        partial_copy(side).wait_recv()
        rows = slice(side * HALF_ROWS, (side + 1) * HALF_ROWS)
        out_ref[rows, :] = (out_ref[rows, :] + rx[side, :, :]) * scale

    for q, owner in ((0, NR // 2 - 1), (1, NR // 2)):
        @pl.when(r == owner)
        def _():
            for k in range(1, NR):
                boundary_copy(q, k).wait_send()

    settle(buf2, NC, s2s)
    settle(buf3, NR, s3s)
    settle(buf4, NC, s4s)
    settle(buf5, NR, s5s)
    for s in range(3):
        for k in range(2):
            over_x(s, k).wait_send()
            for d in range(2):
                own_line(d, s, k).wait_send()
    for s in (1, 2):
        for k in range(2):
            for d in range(2):
                x_line(d, s, k).wait_send()
    for d in range(2):
        own_line(d, 3, d).wait_send()
        x_line(d, 3, d).wait_send()
        partial_copy(d).wait_send()


def shards(old_vectors, pole_values, live_mask, position, rank_weight):
    vmem = pl.BlockSpec(memory_space=pltpu.VMEM)
    v = pltpu.VMEM
    dma = pltpu.SemaphoreType.DMA
    one = dma(())
    return pl.pallas_call(
        kernel,
        out_shape=jax.ShapeDtypeStruct((ROWS, OUT), F32),
        in_specs=[vmem] * 4 + [pl.BlockSpec(memory_space=pltpu.SMEM)],
        out_specs=vmem,
        scratch_shapes=[
            v((2, NZ, ROWS, COLS), F32),
            v((2, 8, 128), F32), v((NC, 8, 128), F32), v((NR, OWN, 128), F32),
            v((NC, 8, 128), F32), v((NR, 8, 128), F32),
            v((OUT, 128), F32), v((OUT, 128), F32),
            v((128, 128), F32), v((128, 128), F32), v((8, 128), F32),
            v((64, 128), F32), v((64, 128), F32), v((64, 128), F32),
            v((OWN, 8192), F32), v((OWN, 128), F32),
            v((ROWS, 2048), BF16), v((ROWS, 2048), BF16),
            v((2048, 3 * OUT), BF16), v((2048, 3 * OUT), BF16),
            v((2, HALF_ROWS, OUT), F32), v((2, HALF_ROWS, OUT), F32), v((OUT, 128), F32),
            dma((2,)), one, one, one, one, one, one, one, one,
            one, dma((2, 4, 2)), dma((2, 4, 2)), dma((3, 2)), dma((3, 2)),
            dma((2, 3, 2)), dma((2, 3, 2)), dma((2,)), dma((2,)), dma((NR - 1,)),
        ],
        compiler_params=pltpu.CompilerParams(
            collective_id=0, has_side_effects=True, vmem_limit_bytes=56 * 2**20
        ),
    )(
        old_vectors,
        pole_values.reshape(64, 128),
        live_mask.reshape(64, 128),
        position.reshape(64, 128),
        rank_weight,
    )


def solution(mesh):
    in_specs = (P("row", "col"), P(), P(), P(), P())
    return jax.shard_map(
        shards, mesh=mesh, in_specs=in_specs, out_specs=P("row", "col"), check_vma=False
    )
```

time: 494 us -> 77.1 us (0.16); the launches traced: 487 us -> 76.9 us
  blocking collectives: 230 us -> 0 us
  local copies, waits for them, and re-layouts: 152 us -> 1.87 us
  Pallas kernels: 0 us -> 74.4 us
  other arithmetic: 65.8 us -> 0 us
  matrix products: 19.3 us -> 0 us
  between operations: 15.6 us -> 0.66 us
    psum x2 -> x0, blocking collectives: 158 us -> none  [the longest x1 132 us: shards(): log_sum = lax.psum(partial_logs, 'col')]
    gather x4 -> x0, local copies, waits for them, and re-layouts: 115 us -> none  [the longest x1 45.5 us: bracket_lengths(): next_gap = pole_values[jnp.minimum(following, order_size - 1)] - pole_values]
    pallas_call x0 -> x1, Pallas kernels: none -> 74.4 us  [shards(): pl.pallas_call(kernel, out_shape=jax.ShapeDtypeStruct((ROWS, OUT), F32),...]
    all_gather x1 -> x0, blocking collectives: 48.6 us -> none  [shards(): edge_rows = lax.all_gather(edge_rows, 'col', axis=1, tiled=True)]
    scatter x1 -> x0, local copies, waits for them, and re-layouts: 30.5 us -> none  [shards(): spread = jnp.zeros((order_size,), jnp.float32).at[position].set(boundary)]
    reduce_sum x74 -> x0, other arithmetic: 28.9 us -> none  [the longest x40 14.8 us: halving(): secular = 1.0 + rank_value * jnp.sum(summands, axis=1)]
    select_n x61 -> x0, other arithmetic: 28.2 us -> none  [the longest x40 26.3 us: halving(): jnp.where(is_below, high_end, middle)]
    unnamed x1 -> x0, blocking collectives: 23.5 us -> none
  transfers between devices with their start and end apart: 1 -> 0, of which waited for: 0 -> 0; matrix products, arithmetic and copies ran while one was open for 45% -> 0% of each run, Pallas kernels for 0% -> 0%
where the time goes in v1:
time: 77.1 us; the launch traced here: 76.9 us
  Pallas kernels  74.4 us (96%)
  local copies, waits for them, and re-layouts  1.87 us (2%)
    pallas_call x1, Pallas kernels, shards(): pl.pallas_call(kernel, out_shape=jax.ShapeDtypeStruct((ROWS, OUT), F32),...  74.4 us
    unnamed x1, local copies, waits for them, and re-layouts  1.87 us

profile of v1, /device:TPU:6, one launch (start us, length us, event | category | flops | bytes accessed | tf_op | source)
XLA Modules:
  0.0 76.9 jit_solution(4662491389470236048)
XLA Ops:
  0.7 74.4 %shard_map.55 = f32[512,256]{1,0:T(8,128)} custom-call(f32[512,128]{1,0:T(8,128)} %x_ref.1, f32[64,128]{1,0:T(8,128)} %bitcast.3, s32[64,128]{1,0:T(8,128)} %bitcast.4, s32[64,128]{1,0:T(8,128)} %bitcast.5, f32[1]{0:T(128)S(6)} %copy.7.rank_ref), custom_call_target="tpu_custom_call" | custom-call | tf_op jit(solution)/shard_map/pallas_call | solution.py:435
  75.1 1.9 %copy.8 = f32[512,256]{1,0:T(8,128)} copy(f32[512,256]{1,0:T(8,128)} %shard_map.55) | data formatting | bytes 1048576

commit v2 on v1

--- a/solution.py
+++ b/solution.py
@@ -12,25 +12,35 @@
 MESH = pl.DeviceIdType.MESH
 FAR = 1e30
 FAR_TEST = 1e29
-ROOT_STEPS = 7
+ROUGH_STEPS, FINE_STEPS = 4, 3
 NR, NC, NZ, NX = 16, 32, 8, 4
 ROWS, COLS = 512, 128
 OUT = 256
 OWN = OUT // NR
 HALF_ROWS = ROWS // 2
+PIECE = HALF_ROWS // 2
 
 
 def reciprocal(x):
     r = pl.reciprocal(x, approx=True)
-    r = r * (2.0 - x * r)
     return r * (2.0 - x * r)
+
+
+def peers(me, n):
+    minor, major = (2, NR // 2) if n == NR else (NX, NZ)
+    steps = [(a, b) for a in range(major) for b in range(minor) if a or b]
+    steps.sort(key=lambda ab: -2 * min(ab[0], major - ab[0]) - min(ab[1], minor - ab[1]))
+    return [
+        lax.rem(me // minor + a, major) * minor + lax.rem(lax.rem(me, minor) + b, minor)
+        for a, b in steps
+    ]
 
 
 def kernel(
     x_ref, pole_ref, live_ref, posn_ref, rank_ref, out_ref,
     panel, buf1, buf2, buf3, buf4, buf5,
     djb, ljb, kp, kd, kl, npole, nsq, nsg, dd, bracket_ref,
-    ah, al, ch, cl, tx, rx, norm_ref,
+    ah, al, ch, cl, tx, rx, norm_ref, sq_ref,
     s1, s2s, s2r, s3s, s3r, s4s, s4r, s5s, s5r,
     own_sem, os, orr, xs, xr, zs, zr, rs, rr, s1s,
 ):
@@ -45,10 +55,10 @@
         return (r, lax.rem(z + dz + NZ, NZ) * NX + lax.rem(x + dx + NX, NX))
 
     barrier = pltpu.get_barrier_semaphore()
-    for k in range(1, NC):
-        pl.semaphore_signal(barrier, inc=1, device_id=(r, lax.rem(c + k, NC)), device_id_type=MESH)
-    for k in range(1, NR):
-        pl.semaphore_signal(barrier, inc=1, device_id=(lax.rem(r + k, NR), c), device_id_type=MESH)
+    for peer in peers(c, NC):
+        pl.semaphore_signal(barrier, inc=1, device_id=(r, peer), device_id_type=MESH)
+    for peer in peers(r, NR):
+        pl.semaphore_signal(barrier, inc=1, device_id=(peer, c), device_id_type=MESH)
 
     own_copy = pltpu.make_async_copy(x_ref, panel.at[0, z], own_sem)
     own_copy.start()
@@ -88,7 +98,7 @@
         src = x_ref.at[pl.ds(ROWS - 8, 8)] if q == 0 else x_ref.at[pl.ds(0, 8)]
         return pltpu.make_async_remote_copy(
             src_ref=src, dst_ref=buf1.at[q], send_sem=s1s.at[k - 1], recv_sem=s1.at[q],
-            device_id=(lax.rem(r + k, NR), c), device_id_type=MESH,
+            device_id=(peers(r, NR)[k - 1], c), device_id_type=MESH,
         )
 
     for q, owner in ((0, NR // 2 - 1), (1, NR // 2)):
@@ -113,7 +123,7 @@
         )
 
     def over_x(i, k):
-        block = lax.rem(z + (0, -1, 1)[i] + NZ, NZ)
+        block = lax.rem(z + (0, -1, 1, -2, 2)[i] + NZ, NZ)
         src = x_ref.at[part(k)] if i == 0 else panel.at[0, block, part(k)]
         return pltpu.make_async_remote_copy(
             src_ref=src, dst_ref=panel.at[1, block, part(k)], send_sem=xs.at[i, k],
@@ -146,9 +156,7 @@
 
     def spread(buf, n, send, recv, along_row):
         me = r if along_row else c
-        order = sorted(range(1, n), key=lambda k: -min(k, n - k))
-        for k in order:
-            peer = lax.rem(me + k, n)
+        for peer in peers(me, n):
             pltpu.make_async_remote_copy(
                 src_ref=buf.at[me], dst_ref=buf.at[me], send_sem=send, recv_sem=recv,
                 device_id=(peer, c) if along_row else (r, peer), device_id_type=MESH,
@@ -169,12 +177,16 @@
         nearest = jnp.minimum(nearest, jnp.where(gap > 0.0, gap, FAR))
     bracket_ref[...] = jnp.broadcast_to(jnp.min(nearest, axis=1, keepdims=True), (OWN, 128))
 
-    for k in range(2):
+    for second in range(2):
         for d in range(2):
+            k = d ^ second
             own_line(d, 0, k).wait_recv()
             own_line(d, 1, k).start()
-        for i in (1, 2):
-            over_x(i, k).start()
+            over_x(1 + d, k).start()
+    for d in range(2):
+        own_line(d, 1, d).wait_recv()
+        own_line(d, 2, d).start()
+        over_x(3 + d, d).start()
 
     settle(buf2, NC, s2r)
 
@@ -192,32 +204,30 @@
     for k in range(64):
         dd[:, k * 128:(k + 1) * 128] = npole[k:k + 1, :] - dj
 
-    def root_step(_, carry):
+    def root_step(inverse, _, carry):
         t, lo, hi = carry
         tb = jnp.broadcast_to(t, (OWN, 128))
         zero = jnp.zeros((OWN, 128), F32)
-        psi, phi, dpsi, dphi = zero, zero, zero, zero
+        value, slope, dpsi = zero, zero, zero
         for k in range(64):
-            q = reciprocal(dd[:, k * 128:(k + 1) * 128] - tb)
+            q = inverse(dd[:, k * 128:(k + 1) * 128] - tb)
             w = nsq[k:k + 1, :] * q
             dw = w * q
-            below = w < 0.0
-            psi = psi + jnp.where(below, w, 0.0)
-            phi = phi + jnp.where(below, 0.0, w)
-            dpsi = dpsi + jnp.where(below, dw, 0.0)
-            dphi = dphi + jnp.where(below, 0.0, dw)
-        psi = jnp.sum(psi, axis=1, keepdims=True)
-        phi = jnp.sum(phi, axis=1, keepdims=True)
+            value = value + w
+            slope = slope + dw
+            dpsi = dpsi + jnp.where(w < 0.0, dw, 0.0)
+        value = jnp.sum(value, axis=1, keepdims=True)
+        slope = jnp.sum(slope, axis=1, keepdims=True)
         dpsi = jnp.sum(dpsi, axis=1, keepdims=True)
-        dphi = jnp.sum(dphi, axis=1, keepdims=True)
-        secular = 1.0 + rho * (psi + phi)
+        dphi = jnp.maximum(slope - dpsi, 0.0)
+        secular = 1.0 + rho * value
         is_below = secular < 0.0
         lo = jnp.where(is_below, t, lo)
         hi = jnp.where(is_below, hi, t)
         e = bracket - t
         lower = rho * t * t * dpsi
         upper = rho * e * e * dphi
-        level = 1.0 + rho * ((psi + t * dpsi) + (phi - e * dphi))
+        level = secular + rho * (t * dpsi - e * dphi)
         linear = level * bracket + lower + upper
         constant = lower * bracket
         side = level * bracket - lower + upper
@@ -231,15 +241,26 @@
         return fresh, lo, hi
 
     start = 0.5 * bracket
-    root, _, _ = lax.fori_loop(0, ROOT_STEPS, root_step, (start, jnp.zeros_like(start), bracket))
+    nothing = jnp.zeros_like(start)
+    rough = functools.partial(root_step, functools.partial(pl.reciprocal, approx=True))
+    root, _, _ = lax.fori_loop(0, ROUGH_STEPS, rough, (start, nothing, bracket))
+    for d in range(2):
+        own_line(d, 1, 1 - d).wait_recv()
+        own_line(d, 2, 1 - d).start()
+    fine = functools.partial(root_step, reciprocal)
+    root, _, _ = lax.fori_loop(0, FINE_STEPS, fine, (root, nothing, bracket))
     own_live = ljb[pl.ds(own_first, OWN), :] > 0.5
     buf3[r, :, :] = jnp.where(own_live, jnp.broadcast_to(root, (OWN, 128)), jnp.broadcast_to(start, (OWN, 128)))
     spread(buf3, NR, s3s, s3r, True)
 
-    for k in range(2):
-        for d in range(2):
-            own_line(d, 1, k).wait_recv()
-            own_line(d, 2, k).start()
+    for d in range(2):
+        own_line(d, 2, d).wait_recv()
+        own_line(d, 3, d).start()
+    for d in range(2):
+        own_line(d, 2, 1 - d).wait_recv()
+        over_x(1 + d, d).wait_recv()
+        over_x(1 + d, 1 - d).wait_recv()
+        x_line(d, 1, 1 - d).start()
 
     settle(buf3, NR, s3r)
 
@@ -261,16 +282,12 @@
     buf4[c, 6:8, :] = jnp.ones((2, 128), F32)
     spread(buf4, NC, s4s, s4r, False)
 
-    own_line(0, 2, 0).wait_recv()
-    own_line(0, 3, 0).start()
-    own_line(1, 2, 1).wait_recv()
-    own_line(1, 3, 1).start()
-    for k in range(2):
-        for d in range(2):
-            over_x(1 + d, k).wait_recv()
-            x_line(d, 1, k).start()
-    own_line(0, 2, 1).wait_recv()
-    own_line(1, 2, 0).wait_recv()
+    for d in range(2):
+        over_x(3 + d, d).wait_recv()
+        x_line(d, 2, d).start()
+    for d in range(2):
+        x_line(d, 1, 1 - d).wait_recv()
+        x_line(d, 2, 1 - d).start()
 
     for b in range(16):
         line = lax.rem(x + 2 * (b // 8), NX)
@@ -304,6 +321,19 @@
                 ch[b * 128:(b + 1) * 128, group * OUT + q * 128:group * OUT + (q + 1) * 128] = hi
                 cl[b * 128:(b + 1) * 128, group * OUT + q * 128:group * OUT + (q + 1) * 128] = lo
 
+    inverse_gaps(0, c, [buf4[c, 4:5, :], buf4[c, 5:6, :]])
+
+    def square_group(g, _):
+        first = pl.multiple_of(g * 8, 8)
+        d_j = djb[pl.ds(first, 8), :]
+        off = buf3[g // 2, pl.ds(pl.multiple_of(lax.rem(g, 2) * 8, 8), 8), :]
+        for k in range(64):
+            w = reciprocal((npole[k:k + 1, :] - d_j) - off)
+            sq_ref[pl.ds(first, 8), k * 128:(k + 1) * 128] = w * w
+        return 0
+
+    lax.fori_loop(0, OUT // 8, square_group, 0)
+
     settle(buf4, NC, s4r)
     product = buf4[0, :, :]
     for k in range(1, NC):
@@ -313,49 +343,39 @@
     buf5[r, :, :] = jnp.sqrt(product / rho)
     spread(buf5, NR, s5s, s5r, True)
 
-    for k in range(2):
-        for d in range(2):
-            x_line(d, 1, k).wait_recv()
-            x_line(d, 2, k).start()
+    for d in range(2):
+        x_line(d, 2, d).wait_recv()
+        x_line(d, 3, d).start()
 
     right = z * NX + lax.rem(x + 1, NX)
     left = z * NX + lax.rem(x + NX - 1, NX)
-    for group, block in ((0, c), (1, right), (2, left)):
+    for group, block in ((1, right), (2, left)):
         inverse_gaps(group, block, [buf4[block, 4:5, :], buf4[block, 5:6, :]])
 
     settle(buf5, NR, s5r)
 
-    def scaled(b):
+    own_copy.wait()
+    for k in range(2):
+        own_line(k, 3, k).wait_recv()
+        over_x(0, k).wait_recv()
+        x_line(k, 2, 1 - k).wait_recv()
+        x_line(k, 3, k).wait_recv()
+
+    hats = []
+    for b in range(16):
         line = lax.rem(x + 2 * (b // 8), NX)
         row = h * NC + (b % 8) * NX + line
         hat = buf5[h * 8 + b % 8, pl.ds(line, 1), :] * nsg[pl.ds(row, 1), :]
-        hat = jnp.where(npole[pl.ds(row, 1), :] < FAR_TEST, hat, 1.0)
-        value = panel[b // 8, b % 8, :, :] * hat
-        hi = value.astype(BF16)
-        ah[:, b * 128:(b + 1) * 128] = hi
-        al[:, b * 128:(b + 1) * 128] = (value - hi.astype(F32)).astype(BF16)
-
-    own_copy.wait()
-    own_line(0, 3, 0).wait_recv()
-    own_line(1, 3, 1).wait_recv()
-    for b in range(8):
-        scaled(b)
-
-    over_x(0, 0).wait_recv()
-    over_x(0, 1).wait_recv()
-    x_line(0, 2, 0).wait_recv()
-    x_line(0, 3, 0).start()
-    x_line(1, 2, 1).wait_recv()
-    x_line(1, 3, 1).start()
-    x_line(0, 2, 1).wait_recv()
-    x_line(1, 2, 0).wait_recv()
-    x_line(0, 3, 0).wait_recv()
-    x_line(1, 3, 1).wait_recv()
-    for b in range(8, 16):
-        scaled(b)
-
-    def product_of(first, count, group):
-        rows = slice(first, first + count)
+        hats.append(jnp.where(npole[pl.ds(row, 1), :] < FAR_TEST, hat, 1.0))
+
+    def scaled(rows):
+        for b in range(16):
+            value = panel[b // 8, b % 8, rows, :] * hats[b]
+            hi = value.astype(BF16)
+            ah[rows, b * 128:(b + 1) * 128] = hi
+            al[rows, b * 128:(b + 1) * 128] = (value - hi.astype(F32)).astype(BF16)
+
+    def product_of(rows, group):
         cols = slice(group * OUT, (group + 1) * OUT)
         a_hi, a_lo = ah[rows, :], al[rows, :]
         c_hi, c_lo = ch[:, cols], cl[:, cols]
@@ -364,28 +384,37 @@
             + jnp.dot(a_lo, c_hi, preferred_element_type=F32)
         ) + jnp.dot(a_hi, c_hi, preferred_element_type=F32)
 
-    def partial_copy(side):
+    def rows_of(side, piece):
+        first = side * HALF_ROWS + piece * PIECE
+        return slice(first, first + PIECE)
+
+    def partial_copy(side, piece):
+        rows = pl.ds(piece * PIECE, PIECE)
         return pltpu.make_async_remote_copy(
-            src_ref=tx.at[side], dst_ref=rx.at[side], send_sem=rs.at[side], recv_sem=rr.at[side],
+            src_ref=tx.at[side, rows], dst_ref=rx.at[side, rows], send_sem=rs.at[side, piece],
+            recv_sem=rr.at[side, piece],
             device_id=col_dev(0, 1 if side == 0 else -1), device_id_type=MESH,
         )
 
-    for side in range(2):
-        tx[side, :, :] = product_of(side * HALF_ROWS, HALF_ROWS, 1 + side)
-        partial_copy(side).start()
-    for side in range(2):
-        out_ref[side * HALF_ROWS:(side + 1) * HALF_ROWS, :] = product_of(side * HALF_ROWS, HALF_ROWS, 0)
+    for piece in range(2):
+        for side in range(2):
+            rows = rows_of(side, piece)
+            scaled(rows)
+            tx[side, piece * PIECE:(piece + 1) * PIECE, :] = product_of(rows, 1 + side)
+            partial_copy(side, piece).start()
+    for piece in range(2):
+        for side in range(2):
+            rows = rows_of(side, piece)
+            out_ref[rows, :] = product_of(rows, 0)
+
+    hat_all = jnp.concatenate([buf5[k, 0:4, :] for k in range(16)], axis=0)
+    nsg[...] = jnp.where(npole[...] < FAR_TEST, hat_all * hat_all, 0.0)
 
     def norm_group(g, _):
         first = pl.multiple_of(g * 8, 8)
-        d_j = djb[pl.ds(first, 8), :]
-        off = buf3[g // 2, pl.ds(pl.multiple_of(lax.rem(g, 2) * 8, 8), 8), :]
         total = jnp.zeros((8, 128), F32)
         for k in range(64):
-            poles = npole[k:k + 1, :]
-            hat = jnp.where(poles < FAR_TEST, buf5[k // 4, k % 4:k % 4 + 1, :], 0.0)
-            w = hat * reciprocal((poles - d_j) - off)
-            total = total + w * w
+            total = total + nsg[k:k + 1, :] * sq_ref[pl.ds(first, 8), k * 128:(k + 1) * 128]
         norm_ref[pl.ds(first, 8), :] = total
         return 0
 
@@ -397,10 +426,12 @@
         scales.append(jnp.where(alive_j, 1.0 / jnp.sqrt(jnp.where(alive_j, square, 1.0)), 1.0))
     scale = jnp.concatenate(scales, axis=1)
 
-    for side in range(2):
-        partial_copy(side).wait_recv()
-        rows = slice(side * HALF_ROWS, (side + 1) * HALF_ROWS)
-        out_ref[rows, :] = (out_ref[rows, :] + rx[side, :, :]) * scale
+    for piece in range(2):
+        for side in range(2):
+            partial_copy(side, piece).wait_recv()
+            rows = rows_of(side, piece)
+            total = out_ref[rows, :] + rx[side, piece * PIECE:(piece + 1) * PIECE, :]
+            out_ref[rows, :] = total * scale
 
     for q, owner in ((0, NR // 2 - 1), (1, NR // 2)):
         @pl.when(r == owner)
@@ -412,19 +443,19 @@
     settle(buf3, NR, s3s)
     settle(buf4, NC, s4s)
     settle(buf5, NR, s5s)
-    for s in range(3):
-        for k in range(2):
-            over_x(s, k).wait_send()
+    for k in range(2):
+        for step in range(3):
+            over_x(step, k).wait_send()
             for d in range(2):
-                own_line(d, s, k).wait_send()
-    for s in (1, 2):
-        for k in range(2):
-            for d in range(2):
-                x_line(d, s, k).wait_send()
-    for d in range(2):
-        own_line(d, 3, d).wait_send()
-        x_line(d, 3, d).wait_send()
-        partial_copy(d).wait_send()
+                own_line(d, step, k).wait_send()
+        own_line(k, 3, k).wait_send()
+        over_x(3 + k, k).wait_send()
+        x_line(k, 1, 1 - k).wait_send()
+        x_line(k, 2, k).wait_send()
+        x_line(k, 2, 1 - k).wait_send()
+        x_line(k, 3, k).wait_send()
+        for piece in range(2):
+            partial_copy(k, piece).wait_send()
 
 
 def shards(old_vectors, pole_values, live_mask, position, rank_weight):
@@ -448,9 +479,10 @@
             v((ROWS, 2048), BF16), v((ROWS, 2048), BF16),
             v((2048, 3 * OUT), BF16), v((2048, 3 * OUT), BF16),
             v((2, HALF_ROWS, OUT), F32), v((2, HALF_ROWS, OUT), F32), v((OUT, 128), F32),
+            v((OUT, 8192), F32),
             dma((2,)), one, one, one, one, one, one, one, one,
-            one, dma((2, 4, 2)), dma((2, 4, 2)), dma((3, 2)), dma((3, 2)),
-            dma((2, 3, 2)), dma((2, 3, 2)), dma((2,)), dma((2,)), dma((NR - 1,)),
+            one, dma((2, 4, 2)), dma((2, 4, 2)), dma((5, 2)), dma((5, 2)),
+            dma((2, 3, 2)), dma((2, 3, 2)), dma((2, 2)), dma((2, 2)), dma((NR - 1,)),
         ],
         compiler_params=pltpu.CompilerParams(
             collective_id=0, has_side_effects=True, vmem_limit_bytes=56 * 2**20

time: 77.1 us -> 68.2 us (0.88)
  Pallas kernels: 74.4 us -> 65.1 us
    pallas_call x1, Pallas kernels: 74.4 us -> 65.1 us  [shards(): pl.pallas_call(kernel, out_shape=jax.ShapeDtypeStruct((ROWS, OUT), F32),...]
where the time goes in v2:
time: 68.2 us; the launch traced here: 67.7 us
  Pallas kernels  65.1 us (95%)
  local copies, waits for them, and re-layouts  1.87 us (3%)
    pallas_call x1, Pallas kernels, shards(): pl.pallas_call(kernel, out_shape=jax.ShapeDtypeStruct((ROWS, OUT), F32),...  65.1 us
    unnamed x1, local copies, waits for them, and re-layouts  1.87 us

profile of v2, /device:TPU:6, one launch (start us, length us, event | category | flops | bytes accessed | tf_op | source)
XLA Modules:
  0.0 67.7 jit_solution(9054108865004157259)
XLA Ops:
  0.7 65.1 %shard_map.55 = f32[512,256]{1,0:T(8,128)} custom-call(f32[512,128]{1,0:T(8,128)} %x_ref.1, f32[64,128]{1,0:T(8,128)} %bitcast.3, s32[64,128]{1,0:T(8,128)} %bitcast.4, s32[64,128]{1,0:T(8,128)} %bitcast.5, f32[1]{0:T(128)S(6)} %copy.7.rank_ref), custom_call_target="tpu_custom_call" | custom-call | tf_op jit(solution)/shard_map/pallas_call | solution.py:466
  65.8 1.9 %copy.8 = f32[512,256]{1,0:T(8,128)} copy(f32[512,256]{1,0:T(8,128)} %shard_map.55) | data formatting | bytes 1048576
